TPU v7x, 256 devices: a whole 4x4x8 slice. The times are simulated.
256 devices in a mesh: depth: 8 (over x_hi, y), res: 32 (over z, x_lo, core).
Axes of the slice: x: 4 (x_hi: 2, x_lo: 2; x = x_hi * 2 + x_lo), y: 4, z: 8, core: 2. Of those that a mesh axis runs over, the one named last changes fastest.
Arguments:
- alignment_left: bfloat16 [2048, 32768], P('depth', 'res'), may hold values from -6 to 6
- alignment_right: bfloat16 [2048, 32768], P('depth', 'res'), may hold values from -6 to 6
- window_starts: int32 [8], replicated, may hold values from 0 to 1016
- outer_product_weight: bfloat16 [1024, 128], replicated, may hold values from -6 to 6
- outer_product_bias: float32 [128], replicated, may hold values from -3 to 3
- query_key_value_gate_weight: bfloat16 [128, 512], replicated, may hold values from -0.5 to 0.5
- output_weight: bfloat16 [128, 128], replicated, may hold values from -2 to 2
- triangle_pair_bias: bfloat16 [4, 1024, 1024], P(None, 'res'), may hold values from -3 to 260
- residue_chain: int32 [1024], replicated, may hold values from 0 to 7, never falling along the last dimension, each value on 1 to 256 neighbouring positions
- interchain_offset: float32 [4], replicated, may hold values from -3 to -0.5
Outputs:
- pair_strip: bfloat16 [64, 1024, 128], P('depth', 'res')
- update: bfloat16 [64, 1024, 128], P('depth', 'res')
All inputs are finite; a program needn't handle non-finite values.
Results may differ from a plain program's by a relative error of at most 0.014.
Values may be sent and summed in bfloat16 or wider, within the bound.
A program may use at most 128 MiB of HBM per device.

v0:
```python
import jax
import jax.numpy as jnp
from jax import lax
from jax.sharding import PartitionSpec as P

PROJ_CHANNELS = 32
CZ = 128
H = 4
DH = 32
R_DEV = 8


epsilon = 1e-05


def layer_norm(values):
    average = jnp.mean(values, axis=-1, keepdims=True)
    centred = values - average
    variance = jnp.mean(centred * centred, axis=-1, keepdims=True)
    return centred * lax.rsqrt(variance + epsilon)


def split_project(flat_outer, weight):
    upper = lax.optimization_barrier(flat_outer.astype(jnp.bfloat16))
    lower = (flat_outer - upper.astype(jnp.float32)).astype(jnp.bfloat16)
    return jnp.dot(upper, weight, preferred_element_type=jnp.float32) + jnp.dot(
        lower, weight, preferred_element_type=jnp.float32
    )


def body(
    alignment_left,
    alignment_right,
    window_starts,
    outer_product_weight,
    outer_product_bias,
    query_key_value_gate_weight,
    output_weight,
    triangle_pair_bias,
    residue_chain,
    interchain_offset,
):
    depth_count = lax.axis_size("depth")
    res_index = lax.axis_index("res")
    sequence_shards = alignment_left.shape[0]
    token_shards = alignment_left.shape[1] // PROJ_CHANNELS
    groups = window_starts.shape[0]
    gathered_rows = groups * R_DEV
    total_seqs = sequence_shards * depth_count
    shard_left = alignment_left.reshape(sequence_shards, token_shards, PROJ_CHANNELS)
    shard_right = alignment_right.reshape(sequence_shards, token_shards, PROJ_CHANNELS)
    row_ids = (window_starts[:, None] + jnp.arange(R_DEV, dtype=jnp.int32)[None, :]).reshape(
        gathered_rows
    )
    first_token = res_index * token_shards
    selector = (
        row_ids[:, None] == first_token + jnp.arange(token_shards, dtype=jnp.int32)[None, :]
    ).astype(jnp.bfloat16)
    shard_rows = jnp.einsum(
        "it,stc->sic", selector, shard_left, preferred_element_type=jnp.float32
    ).astype(jnp.bfloat16)
    alignment_band = lax.psum(
        shard_rows.reshape(sequence_shards, gathered_rows * PROJ_CHANNELS), "res"
    ).astype(jnp.float32)
    alignment_band = alignment_band.astype(jnp.bfloat16).reshape(
        sequence_shards, gathered_rows, PROJ_CHANNELS
    )
    outer_prod = jnp.einsum(
        "hbv,hqz->bqvz", alignment_band, shard_right, preferred_element_type=jnp.float32
    )
    flat_block = outer_prod.reshape(
        R_DEV * lax.axis_size("depth"), token_shards * PROJ_CHANNELS * PROJ_CHANNELS
    ).reshape(R_DEV * lax.axis_size("depth") * token_shards, PROJ_CHANNELS * PROJ_CHANNELS)
    block_out = split_project(flat_block, outer_product_weight)
    projected = lax.psum_scatter(
        block_out.reshape(R_DEV * lax.axis_size("depth"), token_shards * CZ).astype(jnp.bfloat16),
        "depth",
        scatter_dimension=0,
        tiled=True,
    ).astype(jnp.float32)
    pair_strip = (
        projected.reshape(R_DEV * token_shards, CZ) / total_seqs + outer_product_bias[None, :]
    ).astype(jnp.bfloat16)
    pair_strip = pair_strip.reshape(R_DEV, token_shards, CZ)
    normed = layer_norm(pair_strip.astype(jnp.float32)).astype(jnp.bfloat16)
    flat_normed = normed.reshape(R_DEV * token_shards, CZ)
    projection = jnp.dot(
        flat_normed, query_key_value_gate_weight, preferred_element_type=jnp.float32
    ).astype(jnp.bfloat16)
    queries = projection[:, :CZ]
    gate_pre = projection[:, 3 * CZ :]
    kv_local = projection[:, CZ : 3 * CZ].reshape(R_DEV, token_shards, 2 * CZ)
    queries = queries.reshape(R_DEV, token_shards, H, DH)
    own_chain = lax.dynamic_slice_in_dim(residue_chain, first_token, token_shards, 0)
    score_scale = DH ** (-0.5)
    pair_kv = lax.all_gather(kv_local, "res", axis=1, tiled=True)
    run_max = jnp.full((R_DEV, H, token_shards), -jnp.inf, jnp.float32)
    run_sum = jnp.zeros((R_DEV, H, token_shards), jnp.float32)
    run_acc = jnp.zeros((R_DEV, token_shards, CZ), jnp.float32)
    key_count = pair_kv.shape[1]
    key_heads = pair_kv[:, :, :CZ].reshape(R_DEV, key_count, H, DH)
    value_heads = pair_kv[:, :, CZ:].reshape(R_DEV, key_count, H, DH)
    scores = (
        jnp.einsum("rqhd,rkhd->rhqk", queries, key_heads, preferred_element_type=jnp.float32)
        * score_scale
    )
    bias_block = triangle_pair_bias.astype(jnp.float32)
    differ = (own_chain[:, None] != residue_chain[None, :]).astype(jnp.float32)
    scores = scores + (bias_block + interchain_offset[:, None, None] * differ[None, :, :])[None]
    new_max = jnp.max(scores, axis=-1)
    shrink = jnp.exp(run_max - new_max)
    weights = jnp.exp(scores - new_max[..., None])
    new_sum = run_sum * shrink + jnp.sum(weights, axis=-1)
    increment = jnp.einsum(
        "rhqk,rkhd->rqhd",
        weights.astype(jnp.bfloat16),
        value_heads,
        preferred_element_type=jnp.float32,
    ).reshape(R_DEV, token_shards, CZ)
    factor = jnp.repeat(jnp.transpose(shrink, (0, 2, 1)), DH, axis=2)
    run_max, run_sum, run_acc = (new_max, new_sum, run_acc * factor + increment)
    factor_total = jnp.repeat(jnp.transpose(run_sum, (0, 2, 1)), DH, axis=2)
    attended = run_acc / factor_total
    gated_out = (
        jax.nn.sigmoid(gate_pre.astype(jnp.float32)).reshape(R_DEV, token_shards, CZ) * attended
    ).astype(jnp.bfloat16)
    update = jnp.dot(
        gated_out.reshape(R_DEV * token_shards, CZ),
        output_weight,
        preferred_element_type=jnp.float32,
    )
    update = update.astype(jnp.bfloat16).reshape(R_DEV, token_shards, CZ)
    return (pair_strip, update)


def solution(mesh):
    in_specs = (
        P("depth", "res"),
        P("depth", "res"),
        P(),
        P(),
        P(),
        P(),
        P(),
        P(None, "res", None),
        P(),
        P(),
    )
    out_specs = (P("depth", "res", None), P("depth", "res", None))
    return jax.shard_map(body, mesh=mesh, in_specs=in_specs, out_specs=out_specs, check_vma=False)
```

profile of v0, /device:TPU:1, one launch (start us, length us, event | category | flops | bytes accessed | tf_op | source)
XLA Modules:
  0.0 462.8 jit_solution(4600616161007927842)
XLA Ops:
  7.2 1.3 copy.17
  8.6 0.7 iota_add_fusion
  9.4 0.5 fusion.21
  9.9 1.6 copy.38
  11.5 0.2 copy.18
  11.7 230.4 %all-reduce.2.cloned.1.call-done = bf16[256,64,32]{0,2,1:T(8,128)(2,1)} async-done(((bf16[256,64,32]{0,2,1:T(8,128)(2,1)}), bf16[256,64,32]{0,2,1:T(8,128)(2,1)}) %all-reduce.2.cloned.1.call-update) | async-done | bytes 1048592 | tf_op jit(solution)/shard_map/psum | solution.py:62
  242.1 14.4 %convolution_bitcast_fusion = f32[64,32,32,32]{3,2,1,0:T(8,128)} fusion(bf16[256,32,32,1]{0,2,1,3:T(8,128)(2,1)S(1)} %bitcast.50, bf16[256,64,32]{0,2,1:T(8,128)(2,1)} %all-reduce.2.cloned.1.call-done), kind=kOutput, calls=%fused_computation | convolution fusion | flops 1073741824 | bytes 9961472 | tf_op jit(solution)/shard_map/hbv,hqz->bqvz/dot_general | solution.py:68
  256.5 26.1 %reshape_reshape.3 = f32[2048,1024]{1,0:T(8,128)} reshape(f32[64,32,32,32]{3,2,1,0:T(8,128)} %convolution_bitcast_fusion) | data formatting | bytes 16777216 | tf_op jit(solution)/shard_map/reshape;reshape | solution.py:73
  282.6 4.2 convert_element_type.72
  286.8 1.5 copy-done.1
  288.3 1.3 fusion
  289.7 1.3 fusion.4
  291.0 1.0 convert_element_type.76
  292.1 0.2 all-gather.2.cloned.1.call-start
  292.3 73.8 %reduce-scatter.2.cloned.1.call-done = bf16[8,4096]{1,0:T(8,128)(2,1)} async-done(((bf16[64,4096]{1,0:T(8,128)(2,1)}), bf16[8,4096]{1,0:T(8,128)(2,1)}) %reduce-scatter.2.cloned.1.call-update) | async-done | bytes 65552 | tf_op jit(solution)/shard_map/reduce_scatter | solution.py:75
  366.1 0.9 convert_multiply_fusion
  367.2 0.2 fusion.26
  367.5 0.3 convolution_convert_fusion
  367.8 0.7 slice.22
  368.7 0.1 multiply_add_fusion.1
  368.9 0.2 reshape.143
  369.0 67.8 %all-gather.2.cloned.1.call-done = bf16[8,1024,256]{2,1,0:T(8,128)(2,1)} async-done(((bf16[8,32,256]{2,1,0:T(8,128)(2,1)}), bf16[8,1024,256]{2,1,0:T(8,128)(2,1)}) %all-gather.2.cloned.1.call-update) | async-done | bytes 4194320 | tf_op jit(solution)/shard_map/all_gather | solution.py:96
  436.8 4.6 fusion.40
  441.4 2.9 copy.19
  444.3 0.8 fusion.1
  445.1 2.1 copy-done.2
  447.3 1.1 fusion.2
  448.4 2.6 copy.21
  451.0 3.9 fusion.18
  454.9 0.2 copy.22
  455.2 0.3 div.37
  455.4 0.8 convolution_convert_fusion.1
  (39 shorter events, 0.8 us)
Async XLA Ops:
  7.2 279.6 %copy-start = (bf16[1024,128]{1,0:T(8,128)(2,1)S(1)}, bf16[1024,128]{1,0:T(8,128)(2,1)}, u32[]{:S(2)}) copy-start(bf16[1024,128]{1,0:T(8,128)(2,1)} %param.13) | copy-start | bytes 786436
  7.2 4.3 copy-start.4
  7.2 234.9 %all-reduce.2.cloned.1.call-start = ((), (), s32[]{:S(2)}) async-start(), calls=%async_computation.1 | async-start | bytes 2097152 | tf_op jit(solution)/shard_map/psum | solution.py:62
  11.5 354.7 %reduce-scatter.2.cloned.1.call-start = ((), (), s32[]{:S(2)}) async-start(), calls=%async_computation.2 | async-start | bytes 589824 | tf_op jit(solution)/shard_map/reduce_scatter | solution.py:75
  282.6 5.8 %copy-start.1 = (f32[2048,1024]{1,0:T(8,128)S(1)}, f32[2048,1024]{1,0:T(8,128)}, u32[]{:S(2)}) copy-start(f32[2048,1024]{1,0:T(8,128)} %reshape_reshape.3) | copy-start | bytes 25165828
  289.6 77.4 %copy-start.9 = (f32[128]{0:T(128)S(1)}, f32[128]{0:T(128)}, u32[]{:S(2)}) copy-start(f32[128]{0:T(128)} %param.14) | copy-start | bytes 1540
  289.6 77.9 %copy-start.7 = (bf16[128,512]{1,0:T(8,128)(2,1)S(1)}, bf16[128,512]{1,0:T(8,128)(2,1)}, u32[]{:S(2)}) copy-start(bf16[128,512]{1,0:T(8,128)(2,1)} %param.15) | copy-start | bytes 393220
  289.7 78.9 %copy-start.8 = (s32[1024]{0:T(1024)S(1)}, s32[1024]{0:T(1024)}, u32[]{:S(2)}) copy-start(s32[1024]{0:T(1024)} %param.18) | copy-start | bytes 12292
  289.7 79.0 %copy-start.5 = (bf16[4,32,1024]{2,1,0:T(8,128)(2,1)S(1)}, bf16[4,32,1024]{2,1,0:T(8,128)(2,1)}, u32[]{:S(2)}) copy-start(bf16[4,32,1024]{2,1,0:T(8,128)(2,1)} %param.17) | copy-start | bytes 786436
  289.7 79.0 %copy-start.10 = (f32[4]{0:T(128)S(1)}, f32[4]{0:T(128)}, u32[]{:S(2)}) copy-start(f32[4]{0:T(128)} %param.19) | copy-start | bytes 52
  292.1 144.7 %all-gather.2.cloned.1.call-start = ((), (), s32[]{:S(2)}) async-start(), calls=%async_computation.3 | async-start | bytes 4325376 | tf_op jit(solution)/shard_map/all_gather | solution.py:96
  367.1 74.3 %copy-start.6 = (bf16[8,32,128]{2,1,0:T(8,128)(2,1)}, bf16[8,32,128]{2,1,0:T(8,128)(2,1)S(1)}, u32[]{:S(2)}) copy-start(bf16[8,32,128]{2,1,0:T(8,128)(2,1)S(1)} %get-tuple-element.3) | copy-start | bytes 196612
  445.1 2.1 copy-start.2
  445.1 3.3 copy-start.3
  451.0 4.5 copy-start.11
Sparse Core Ops, SparseCore 0:
  11.6 230.4 all-reduce.1
  292.2 73.8 reduce-scatter.1
  368.6 68.1 all-gather.1
where the time goes:
time: 463 us
  waiting for transfers between devices  372 us (80%)
  local copies, waits for them, and re-layouts  45.7 us (10%)
  matrix products  23.3 us (5%)
  between operations  14 us (3%)
  other arithmetic  7.4 us (2%)
    psum x1, waiting for transfers between devices, body(): lax.psum(shard_rows.reshape(sequence_shards, gathered_rows * PROJ_CHANNEL...  230 us
    reduce_scatter x1, waiting for transfers between devices, body(): lax.psum_scatter(block_out.reshape(R_DEV * lax.axis_size('depth'), token_...  73.8 us
    all_gather x1, waiting for transfers between devices, body(): pair_kv = lax.all_gather(kv_local, 'res', axis=1, tiled=True)  67.8 us
    another operation x1, local copies, waits for them, and re-layouts, body(): flat_block = outer_prod.reshape(R_DEV * lax.axis_size('depth'), token_sha...  26.1 us
    dot_general x1, matrix products, body(): jnp.einsum('hbv,hqz->bqvz', alignment_band, shard_right, preferred_elemen...  14.4 us
  transfers between devices with their start and end apart: 3, of which 3 were waited for; matrix products, arithmetic and copies ran while one was open for 0% of the time, Pallas kernels for 0%

commit v1 on v0

v1 whole, which is shorter than its diff:
```python
import functools

import jax
import jax.numpy as jnp
from jax import lax
from jax.experimental import pallas as pl
from jax.experimental.pallas import tpu as pltpu
from jax.sharding import PartitionSpec as P

CH = 32
CZ = 128
H = 4
DH = 32
U = 8
EPS = 1e-05
MESH = pl.DeviceIdType.MESH
f32 = jnp.float32
bf16 = jnp.bfloat16


def dot(a, b):
    return jnp.dot(a, b, preferred_element_type=f32)


def dot_t(a, b):
    return lax.dot_general(a, b, (((1,), (1,)), ((), ())), preferred_element_type=f32)


def kernel(
    nd,
    nr,
    seqs,
    ws_ref,
    off_ref,
    left_ref,
    right_ref,
    w_ref,
    ob_ref,
    wqkvg_ref,
    wout_ref,
    tb_ref,
    chain_ref,
    pair_ref,
    upd_ref,
    l1,
    l1_tiles,
    sel_own,
    sel_in,
    band,
    r_t,
    r_p,
    w_f,
    wbd,
    bias_f,
    xs,
    part,
    rs_in,
    nb,
    qp,
    s0_s,
    s0_r,
    sx_s,
    sx_r,
    bz_s,
    bz_r,
    bx_s,
    bx_r,
    bc_s,
    bc_r,
    rs_s,
    rs_r,
    nz_s,
    nz_r,
    nx_s,
    nx_r,
    nc_s,
    nc_r,
):
    nz = nr // 4
    nm = nr // 2
    chunk = seqs // nm
    tok = left_ref.shape[1] // CH
    groups = nd
    gh = groups // 2
    half = gh * U * CH
    tiles_dev = left_ref.shape[1] // 128
    keys = nr * tok

    d = lax.axis_index("depth")
    r = lax.axis_index("res")
    z = r // 4
    x = (r // 2) % 2
    c = r % 2
    m = r // 2
    x_peer = z * 4 + (1 - x) * 2 + c
    c_peer = z * 4 + x * 2 + (1 - c)

    def remote(src, dst, send, recv, depth, res):
        return pltpu.make_async_remote_copy(
            src_ref=src,
            dst_ref=dst,
            send_sem=send,
            recv_sem=recv,
            device_id=(depth, res),
            device_id_type=MESH,
        )

    barrier = pltpu.get_barrier_semaphore()

    @pl.loop(1, nm)
    def _(k):
        other = lax.rem(m + k, nm)
        pl.semaphore_signal(barrier, inc=1, device_id=(d, other * 2 + c), device_id_type=MESH)

    @pl.loop(1, nd)
    def _(k):
        pl.semaphore_signal(barrier, inc=1, device_id=(lax.rem(d + k, nd), r), device_id_type=MESH)

    pl.semaphore_signal(barrier, inc=1, device_id=(d, c_peer), device_id_type=MESH)
    pl.semaphore_wait(barrier, nm - 1 + nd - 1 + 1)

    def scatter_copy(k):
        other = lax.rem(m + k, nm)
        return remote(
            left_ref.at[pl.ds(other * chunk, chunk), :],
            l1.at[m],
            s0_s.at[k],
            s0_r.at[k],
            d,
            other * 2 + c,
        )

    @pl.loop(1, nm)
    def _(k):
        scatter_copy(k).start()

    l1[m] = left_ref[pl.ds(pl.multiple_of(m * chunk, chunk), chunk), :]

    for q in range(seqs // 128):
        r_t[q] = jnp.transpose(right_ref[q * 128 : (q + 1) * 128, :].astype(f32))
    w_f[...] = w_ref[...].astype(f32)
    wbd[...] = jnp.zeros_like(wbd)
    for i in range(CH):
        for q in range(seqs // 128):
            r_p[i * tok : (i + 1) * tok, q * 128 : (q + 1) * 128] = r_t[
                q, pl.ds(i, tok, stride=CH), :
            ].astype(bf16)
        w_i = w_f[pl.ds(i, CH, stride=CH), :].astype(bf16)
        for b in range(4):
            wbd[i * 128 + b * CH : i * 128 + (b + 1) * CH, b * CZ : (b + 1) * CZ] = w_i

    chain = chain_ref[...]
    key_at = lax.broadcasted_iota(jnp.int32, (tok, keys), 1)
    query_at = lax.broadcasted_iota(jnp.int32, (tok, keys), 0) + r * tok
    own = jnp.sum(jnp.where(key_at == query_at, chain, 0).astype(f32), axis=1, keepdims=True)
    differ = (own != chain.astype(f32)).astype(f32)
    for h in range(H):
        bias_f[h * tok : (h + 1) * tok, :] = tb_ref[h].astype(f32) + off_ref[h] * differ

    @pl.loop(1, nm)
    def _(k):
        scatter_copy(k).wait()

    for i in range(nm):
        for t in range(tiles_dev):
            l1_tiles[i * tiles_dev + t] = l1[i, :, t * 128 : (t + 1) * 128]

    last_tile = nr * tiles_dev - 1
    for g in range(groups):
        start = ws_ref[g]
        first = lax.div(start, 4)
        shift = start - 4 * first
        pieces = []
        for t in range(3):
            tile = jnp.minimum(first + t, last_tile)
            src = lax.div(tile, tiles_dev)
            chip = lax.div(src, 2)
            piece = l1_tiles[chip * tiles_dev + tile - src * tiles_dev].astype(f32)
            pieces.append(jnp.where(src - 2 * chip == c, piece, 0.0))
        wide = jnp.concatenate(pieces, axis=1)
        picked = wide[:, :256]
        for b in range(1, 4):
            picked = jnp.where(shift == b, wide[:, b * CH : b * CH + 256], picked)
        sel_own[g // gh, :, (g % gh) * 256 : (g % gh + 1) * 256] = picked.astype(bf16)

    swap = remote(sel_own.at[1 - c], sel_in, sx_s, sx_r, d, c_peer)
    swap.start()
    swap.wait()
    band[c, pl.ds(pl.multiple_of(m * chunk, chunk), chunk), :] = (
        sel_own[c].astype(f32) + sel_in[...].astype(f32)
    ).astype(bf16)

    def gather(block, z_s, z_r, x_s, x_r, c_s, c_r):
        def to_z(k):
            zz = lax.rem(z + k, nz)
            ref = block(r)
            return remote(ref, ref, z_s.at[k], z_r.at[k], d, zz * 4 + x * 2 + c)

        def to_x(k):
            ref = block(lax.rem(z + nz - k, nz) * 4 + x * 2 + c)
            return remote(ref, ref, x_s.at[k], x_r.at[k], d, x_peer)

        def to_c(k):
            zz = lax.rem(z + nz - lax.rem(k, nz), nz)
            xx = lax.rem(x + k // nz, 2)
            ref = block(zz * 4 + xx * 2 + c)
            return remote(ref, ref, c_s.at[k], c_r.at[k], d, c_peer)

        def begin():
            @pl.loop(1, nz)
            def _(k):
                to_z(k).start()

            to_x(0).start()
            to_c(0).start()

        def finish_own():
            @pl.loop(1, nz)
            def _(i):
                k = lax.rem(i, 2) * ((i + 1) // 2) + (1 - lax.rem(i, 2)) * (nz - i // 2)
                to_z(k).wait_recv()
                to_x(k).start()
                to_c(k).start()

            @pl.loop(0, nz)
            def _(k):
                to_x(k).wait_recv()
                to_c(nz + k).start()

        def finish_other():
            @pl.loop(0, 2 * nz)
            def _(k):
                to_c(k).wait_recv()

        def drain():
            @pl.loop(1, nz)
            def _(k):
                to_z(k).wait_send()

            @pl.loop(0, nz)
            def _(k):
                to_x(k).wait_send()

            @pl.loop(0, 2 * nz)
            def _(k):
                to_c(k).wait_send()

        return begin, finish_own, finish_other, drain

    begin, finish_own, finish_other, drain_band = gather(
        lambda res: band.at[res % 2, pl.ds((res // 2) * chunk, chunk), :],
        bz_s,
        bz_r,
        bx_s,
        bx_r,
        bc_s,
        bc_r,
    )
    begin()
    finish_own()

    def reduce_copy(g):
        return remote(part.at[g], rs_in.at[d], rs_s.at[g], rs_r.at[d], g, r)

    def outer(side):
        for i in range(gh):
            y = dot(r_p[...], band[side, :, i * 256 : (i + 1) * 256]).astype(bf16)
            for t in range(2):
                for e in range(CH):
                    row = (2 * i + t) * tok
                    xs[row : row + tok, e * 128 : (e + 1) * 128] = y[
                        e * tok : (e + 1) * tok, t * 128 : (t + 1) * 128
                    ]
        out = dot(xs[...], wbd[...]).astype(bf16)
        for i in range(gh):
            g = side * gh + i
            for u in range(U):
                row = (2 * i + u // 4) * tok
                part[g, u * tok : (u + 1) * tok, :] = out[
                    row : row + tok, (u % 4) * CZ : (u % 4 + 1) * CZ
                ]

            @pl.when(g != d)
            def _():
                reduce_copy(g).start()

    outer(c)
    finish_other()
    outer(1 - c)
    rs_in[d] = part[d]

    @pl.loop(1, nd)
    def _(k):
        src = lax.rem(d + k, nd)
        remote(part.at[src], rs_in.at[src], rs_s.at[src], rs_r.at[src], src, r).wait()

    total = rs_in[0].astype(f32)
    for k in range(1, nd):
        total = total + rs_in[k].astype(f32)
    pair = (total * (1.0 / (seqs * nd)) + ob_ref[...]).astype(bf16)
    pair_ref[...] = pair.reshape(U, tok, CZ)
    value = pair.astype(f32)
    centred = value - jnp.mean(value, axis=1, keepdims=True)
    variance = jnp.mean(centred * centred, axis=1, keepdims=True)
    normed = (centred * lax.rsqrt(variance + EPS)).astype(bf16)
    nb[:, pl.ds(pl.multiple_of(r * tok, tok), tok), :] = normed.reshape(U, tok, CZ)

    begin, finish_own, finish_other, drain_normed = gather(
        lambda res: nb.at[:, pl.ds(res * tok, tok), :],
        nz_s,
        nz_r,
        nx_s,
        nx_r,
        nc_s,
        nc_r,
    )
    begin()
    queries = dot(normed, wqkvg_ref[:, :CZ]).astype(bf16)
    gate = jax.nn.sigmoid(dot(normed, wqkvg_ref[:, 3 * CZ :]).astype(bf16).astype(f32))
    head_of = lax.broadcasted_iota(jnp.int32, (U * tok, CZ), 1) // DH
    for h in range(H):
        own_head = jnp.where(head_of == h, queries, jnp.zeros_like(queries))
        key_side = (dot_t(own_head, wqkvg_ref[:, CZ : 2 * CZ]) * (DH**-0.5)).astype(bf16)
        for u in range(U):
            qp[u, h * tok : (h + 1) * tok, :] = key_side[u * tok : (u + 1) * tok, :]
    finish_own()
    finish_other()

    head_lane = lax.broadcasted_iota(jnp.int32, (tok, CZ), 1) // DH
    for u in range(U):
        rows = nb[u]
        scores = dot_t(qp[u], rows) + bias_f[...]
        top = jnp.max(scores, axis=1, keepdims=True)
        weights = jnp.exp(scores - top)
        denom = jnp.sum(weights, axis=1, keepdims=True)
        mixed = dot(weights.astype(bf16), rows) / denom
        values = dot(mixed.astype(bf16), wqkvg_ref[:, 2 * CZ : 3 * CZ])
        attended = jnp.zeros((tok, CZ), f32)
        for h in range(H):
            attended = jnp.where(head_lane == h, values[h * tok : (h + 1) * tok, :], attended)
        gated = (gate[u * tok : (u + 1) * tok, :] * attended).astype(bf16)
        upd_ref[u] = dot(gated, wout_ref[...]).astype(bf16)

    drain_band()
    drain_normed()


def body(
    nd,
    nr,
    alignment_left,
    alignment_right,
    window_starts,
    outer_product_weight,
    outer_product_bias,
    query_key_value_gate_weight,
    output_weight,
    triangle_pair_bias,
    residue_chain,
    interchain_offset,
):
    seqs, cols = alignment_left.shape
    tok = cols // CH
    nz, nm = nr // 4, nr // 2
    chunk = seqs // nm
    half = (nd // 2) * U * CH
    keys = nr * tok
    vmem = pl.BlockSpec(memory_space=pltpu.VMEM)
    smem = pl.BlockSpec(memory_space=pltpu.SMEM)
    sem = pltpu.SemaphoreType.DMA
    out = jax.ShapeDtypeStruct((U, tok, CZ), bf16)
    return pl.pallas_call(
        functools.partial(kernel, nd, nr, seqs),
        out_shape=(out, out),
        in_specs=[smem, smem] + [vmem] * 8,
        out_specs=(vmem, vmem),
        scratch_shapes=[
            pltpu.VMEM((nm, chunk, cols), bf16),
            pltpu.VMEM((nm * cols // 128, chunk, 128), bf16),
            pltpu.VMEM((2, chunk, half), bf16),
            pltpu.VMEM((chunk, half), bf16),
            pltpu.VMEM((2, seqs, half), bf16),
            pltpu.VMEM((seqs // 128, cols, 128), f32),
            pltpu.VMEM((cols, seqs), bf16),
            pltpu.VMEM((CH * CH, CZ), f32),
            pltpu.VMEM((CH * 128, 4 * CZ), bf16),
            pltpu.VMEM((H * tok, keys), f32),
            pltpu.VMEM((nd // 2 * 2 * tok, CH * 128), bf16),
            pltpu.VMEM((nd, U * tok, CZ), bf16),
            pltpu.VMEM((nd, U * tok, CZ), bf16),
            pltpu.VMEM((U, keys, CZ), bf16),
            pltpu.VMEM((U, H * tok, CZ), bf16),
            sem((nm,)),
            sem((nm,)),
            sem,
            sem,
            sem((nz,)),
            sem((nz,)),
            sem((nz,)),
            sem((nz,)),
            sem((2 * nz,)),
            sem((2 * nz,)),
            sem((nd,)),
            sem((nd,)),
            sem((nz,)),
            sem((nz,)),
            sem((nz,)),
            sem((nz,)),
            sem((2 * nz,)),
            sem((2 * nz,)),
        ],
        compiler_params=pltpu.CompilerParams(
            collective_id=0, has_side_effects=True, vmem_limit_bytes=50 * 1024 * 1024
        ),
        cost_estimate=pl.CostEstimate(
            flops=4_000_000_000, bytes_accessed=4_000_000, transcendentals=1_100_000
        ),
    )(
        window_starts,
        interchain_offset,
        alignment_left,
        alignment_right,
        outer_product_weight,
        outer_product_bias.reshape(1, CZ),
        query_key_value_gate_weight,
        output_weight,
        triangle_pair_bias,
        residue_chain.reshape(1, keys),
    )


def solution(mesh):
    in_specs = (
        P("depth", "res"),
        P("depth", "res"),
        P(),
        P(),
        P(),
        P(),
        P(),
        P(None, "res", None),
        P(),
        P(),
    )
    out_specs = (P("depth", "res", None), P("depth", "res", None))
    return jax.shard_map(
        functools.partial(body, mesh.shape["depth"], mesh.shape["res"]),
        mesh=mesh,
        in_specs=in_specs,
        out_specs=out_specs,
        check_vma=False,
    )
```

time: 463 us -> 91.8 us (0.20)
  waiting for transfers between devices: 372 us -> 0 us
  Pallas kernels: 0 us -> 82.3 us
  local copies, waits for them, and re-layouts: 45.7 us -> 8.25 us
  matrix products: 23.3 us -> 0 us
  between operations: 14 us -> 0.67 us
  other arithmetic: 7.4 us -> 0 us
    psum x1 -> x0, waiting for transfers between devices: 230 us -> none  [body(): lax.psum(shard_rows.reshape(sequence_shards, gathered_rows * PROJ_CHANNEL...]
    pallas_call x0 -> x1, Pallas kernels: none -> 82.3 us  [body(): pl.pallas_call(functools.partial(kernel, nd, nr, seqs), out_shape=(out, o...]
    reduce_scatter x1 -> x0, waiting for transfers between devices: 73.8 us -> none  [body(): lax.psum_scatter(block_out.reshape(R_DEV * lax.axis_size('depth'), token_...]
    all_gather x1 -> x0, waiting for transfers between devices: 67.8 us -> none  [body(): pair_kv = lax.all_gather(kv_local, 'res', axis=1, tiled=True)]
    another operation x1 -> x0, local copies, waits for them, and re-layouts: 26.1 us -> none  [body(): flat_block = outer_prod.reshape(R_DEV * lax.axis_size('depth'), token_sha...]
    dot_general x8 -> x0, matrix products: 23.3 us -> none  [the longest x1 14.4 us: body(): jnp.einsum('hbv,hqz->bqvz', alignment_band, shard_right, preferred_elemen...]
    slice x5 -> x0, local copies, waits for them, and re-layouts: 10.8 us -> none  [the longest x2 7.48 us: body(): key_heads = pair_kv[:, :, :CZ].reshape(R_DEV, key_count, H, DH)]
  transfers between devices with their start and end apart: 3 -> 0, of which waited for: 3 -> 0; matrix products, arithmetic and copies ran while one was open for 0% -> 0% of each run, Pallas kernels for 0% -> 0%
where the time goes in v1:
time: 91.8 us; the launch traced here: 91.3 us
  Pallas kernels  82.3 us (90%)
  local copies, waits for them, and re-layouts  8.25 us (9%)
    pallas_call x1, Pallas kernels, body(): pl.pallas_call(functools.partial(kernel, nd, nr, seqs), out_shape=(out, o...  82.3 us
    unnamed x22, local copies, waits for them, and re-layouts  8.25 us

profile of v1, /device:TPU:1, one launch (start us, length us, event | category | flops | bytes accessed | tf_op | source)
XLA Modules:
  0.0 91.3 jit_solution(17718493320994979457)
XLA Ops:
  0.6 0.0 copy-start.7
  0.6 0.0 copy-start.8
  0.7 0.0 copy-start.9
  0.7 0.6 copy-done.7
  1.3 0.0 copy-done.8
  1.3 0.0 copy-done.9
  1.3 0.0 copy-start
  1.3 1.0 %copy-done = bf16[256,1024]{1,0:T(8,128)(2,1)S(1)} copy-done((bf16[256,1024]{1,0:T(8,128)(2,1)S(1)}, bf16[256,1024]{1,0:T(8,128)(2,1)}, u32[]{:S(2)}) %copy-start) | copy-done | bytes 524312
  2.4 0.0 copy-start.1
  2.4 1.0 %copy-done.1 = bf16[256,1024]{1,0:T(8,128)(2,1)S(1)} copy-done((bf16[256,1024]{1,0:T(8,128)(2,1)S(1)}, bf16[256,1024]{1,0:T(8,128)(2,1)}, u32[]{:S(2)}) %copy-start.1) | copy-done | bytes 524312
  3.4 0.0 copy-start.2
  3.4 0.9 %copy-done.2 = bf16[1024,128]{1,0:T(8,128)(2,1)S(1)} copy-done((bf16[1024,128]{1,0:T(8,128)(2,1)S(1)}, bf16[1024,128]{1,0:T(8,128)(2,1)}, u32[]{:S(2)}) %copy-start.2) | copy-done | bytes 262168
  4.4 0.0 copy-start.3
  4.4 0.9 %copy-done.3 = bf16[4,32,1024]{2,1,0:T(8,128)(2,1)S(1)} copy-done((bf16[4,32,1024]{2,1,0:T(8,128)(2,1)S(1)}, bf16[4,32,1024]{2,1,0:T(8,128)(2,1)}, u32[]{:S(2)}) %copy-start.3) | copy-done | bytes 262168
  5.3 0.0 copy-start.4
  5.3 0.9 copy-done.4
  6.2 0.0 copy-start.5
  6.2 0.8 copy-done.5
  7.0 0.0 copy-start.6
  7.0 0.7 copy-done.6
  7.7 82.3 %shard_map.113 = (bf16[8,32,128]{2,1,0:T(8,128)(2,1)S(1)}, bf16[8,32,128]{2,1,0:T(8,128)(2,1)S(1)}) custom-call(s32[8]{0:T(128)S(1)} %copy-done.7, f32[4]{0:T(128)S(1)} %copy-done.8, bf16[256,1024]{1,0:T(8,128)(2,1)S(1)} %copy-done, bf16[256,1024]{1,0:T(8,128)(2,1)S(1)} %copy-done.1, bf16[1024,128]{1,0:T(8,128)(2,1)S(1)} %copy-done.2, f32[1,128]{1,0:T(1,128)S(1)} %bitcast.3, ...), custom_call_target="tpu_custom_call" | custom-call | flops 4000000000 | bytes 4000000 | tf_op jit(solution)/shard_map/pallas_call | solution.py:372
  90.0 0.6 copy.14
  90.6 0.6 copy.15
Async XLA Ops:
  0.6 0.7 copy-start.7
  0.6 0.7 copy-start.8
  0.7 0.7 copy-start.9
  1.3 1.0 %copy-start = (bf16[256,1024]{1,0:T(8,128)(2,1)S(1)}, bf16[256,1024]{1,0:T(8,128)(2,1)}, u32[]{:S(2)}) copy-start(bf16[256,1024]{1,0:T(8,128)(2,1)} %left_ref.1) | copy-start | bytes 1572868
  2.4 1.0 %copy-start.1 = (bf16[256,1024]{1,0:T(8,128)(2,1)S(1)}, bf16[256,1024]{1,0:T(8,128)(2,1)}, u32[]{:S(2)}) copy-start(bf16[256,1024]{1,0:T(8,128)(2,1)} %right_ref.1) | copy-start | bytes 1572868
  3.4 0.9 %copy-start.2 = (bf16[1024,128]{1,0:T(8,128)(2,1)S(1)}, bf16[1024,128]{1,0:T(8,128)(2,1)}, u32[]{:S(2)}) copy-start(bf16[1024,128]{1,0:T(8,128)(2,1)} %w_ref.1) | copy-start | bytes 786436
  4.4 0.9 %copy-start.3 = (bf16[4,32,1024]{2,1,0:T(8,128)(2,1)S(1)}, bf16[4,32,1024]{2,1,0:T(8,128)(2,1)}, u32[]{:S(2)}) copy-start(bf16[4,32,1024]{2,1,0:T(8,128)(2,1)} %tb_ref.1) | copy-start | bytes 786436
  5.3 0.9 copy-start.4
  6.2 0.8 copy-start.5
  7.0 0.7 copy-start.6

commit v2 on v1

v2 whole, which is shorter than its diff:
```python
import functools

import jax
import jax.numpy as jnp
from jax import lax
from jax.experimental import pallas as pl
from jax.experimental.pallas import tpu as pltpu
from jax.sharding import PartitionSpec as P

CH = 32
CZ = 128
H = 4
DH = 32
U = 8
EPS = 1e-05
VMEM_BYTES = 63 * 1024 * 1024
MESH = pl.DeviceIdType.MESH
f32 = jnp.float32
bf16 = jnp.bfloat16


def dot(a, b):
    return jnp.dot(a, b, preferred_element_type=f32)


def dot_t(a, b):
    return lax.dot_general(a, b, (((1,), (1,)), ((), ())), preferred_element_type=f32)


def kernel(
    nd,
    nr,
    ws_ref,
    off_ref,
    left_hbm,
    right_hbm,
    w_hbm,
    ob_hbm,
    wqkvg_hbm,
    wout_hbm,
    tb_hbm,
    chain_hbm,
    pair_ref,
    upd_ref,
    right,
    w,
    ob,
    wqkvg,
    wout,
    chain_v,
    tb,
    l1,
    l1_tiles,
    picks,
    picks_in,
    band,
    r_t,
    r_p,
    w_f,
    wbd,
    bias_f,
    xs,
    part,
    rs_in,
    rows_out,
    nb,
    ub,
    upd_in,
    in_sem,
    s0_s,
    s0_r,
    tb_s,
    tb_r,
    pk_s,
    pk_r,
    bz_s,
    bz_r,
    bx_s,
    bx_r,
    bc_s,
    bc_r,
    rs_s,
    rs_r,
    ex_s,
    ex_r,
    nz_s,
    nz_r,
    up_s,
    up_r,
):
    seqs, cols = left_hbm.shape
    tok = cols // CH
    nz = nr // 4
    hops = nz // 2
    chunk = seqs // nz
    groups = nd
    quarter = groups // 4 * U * CH
    gq = groups // 4
    tiles_dev = cols // 128
    keys = nr * tok
    level = 4 * tok

    d = lax.axis_index("depth")
    r = lax.axis_index("res")
    z = r // 4
    p = r % 4
    x = p // 2
    c = p % 2
    p_x = (1 - x) * 2 + c
    p_c = x * 2 + (1 - c)
    p_xc = (1 - x) * 2 + (1 - c)

    def remote(src, dst, send, recv, depth, res):
        return pltpu.make_async_remote_copy(
            src_ref=src,
            dst_ref=dst,
            send_sem=send,
            recv_sem=recv,
            device_id=(depth, res),
            device_id_type=MESH,
        )

    barrier = pltpu.get_barrier_semaphore()
    others = (p_x, p_c, p_xc)
    for k in range(1, nz):
        pl.semaphore_signal(
            barrier, inc=1, device_id=(d, lax.rem(z + k, nz) * 4 + p), device_id_type=MESH
        )
    for q in others:
        pl.semaphore_signal(barrier, inc=1, device_id=(d, z * 4 + q), device_id_type=MESH)
    for k in range(1, nd):
        pl.semaphore_signal(barrier, inc=1, device_id=(lax.rem(d + k, nd), r), device_id_type=MESH)

    inputs = [
        pltpu.make_async_copy(src, dst, in_sem.at[i])
        for i, (src, dst) in enumerate(
            (
                (right_hbm, right),
                (w_hbm, w),
                (ob_hbm, ob),
                (wqkvg_hbm, wqkvg),
                (wout_hbm, wout),
                (chain_hbm, chain_v),
                (tb_hbm, tb.at[p]),
                (left_hbm.at[pl.ds(z * chunk, chunk), :], l1.at[z]),
            )
        )
    ]
    for copy in inputs:
        copy.start()
    pl.semaphore_wait(barrier, nz - 1 + 3 + nd - 1)

    def scatter_copy(k):
        zz = lax.rem(z + k, nz)
        return remote(
            left_hbm.at[pl.ds(zz * chunk, chunk), :],
            l1.at[z],
            s0_s.at[k],
            s0_r.at[k],
            d,
            zz * 4 + p,
        )

    order = sorted(range(1, nz), key=lambda k: -min(k, nz - k))
    for k in order:
        scatter_copy(k).start()

    for copy in inputs:
        copy.wait()
    tb_own_x = remote(tb.at[p], tb.at[p], tb_s.at[0], tb_r.at[0], d, z * 4 + p_x)
    tb_own_c = remote(tb.at[p], tb.at[p], tb_s.at[1], tb_r.at[1], d, z * 4 + p_c)
    tb_x_c = remote(tb.at[p_x], tb.at[p_x], tb_s.at[2], tb_r.at[2], d, z * 4 + p_c)
    tb_own_x.start()
    tb_own_c.start()

    for q in range(seqs // 128):
        r_t[q] = jnp.transpose(right[q * 128 : (q + 1) * 128, :].astype(f32))
    w_f[...] = w[...].astype(f32)
    wbd[...] = jnp.zeros_like(wbd)
    for i in range(CH):
        for q in range(seqs // 128):
            r_p[i * tok : (i + 1) * tok, q * 128 : (q + 1) * 128] = r_t[
                q, pl.ds(i, tok, stride=CH), :
            ].astype(bf16)
        w_i = w_f[pl.ds(i, CH, stride=CH), :].astype(bf16)
        for b in range(4):
            wbd[i * 128 + b * CH : i * 128 + (b + 1) * CH, b * CZ : (b + 1) * CZ] = w_i

    for k in order:
        scatter_copy(k).wait()

    for i in range(nz):
        for t in range(tiles_dev):
            l1_tiles[i * tiles_dev + t] = l1[i, :, t * 128 : (t + 1) * 128]

    last_tile = nr * tiles_dev - 1
    for g in range(groups):
        start = ws_ref[g]
        first = lax.div(start, 4)
        shift = start - 4 * first
        pieces = []
        for t in range(3):
            tile = jnp.minimum(first + t, last_tile)
            src = lax.div(tile, tiles_dev)
            zz = lax.div(src, 4)
            piece = l1_tiles[zz * tiles_dev + tile - src * tiles_dev].astype(f32)
            pieces.append(jnp.where(src - 4 * zz == p, piece, 0.0))
        wide = jnp.concatenate(pieces, axis=1)
        picked = wide[:, :256]
        for b in range(1, 4):
            picked = jnp.where(shift == b, wide[:, b * CH : b * CH + 256], picked)
        picks[g // gq, :, (g % gq) * 256 : (g % gq + 1) * 256] = picked.astype(bf16)

    picks_out = [
        remote(picks.at[q], picks_in.at[p], pk_s.at[q], pk_r.at[p], d, z * 4 + q) for q in others
    ]
    for copy in picks_out:
        copy.start()
    tb_own_x.wait_recv()
    tb_x_c.start()
    for q, copy in zip(others, picks_out):
        copy.wait_send()
        remote(picks.at[q], picks_in.at[q], pk_s.at[q], pk_r.at[q], d, z * 4 + q).wait_recv()
    picks_in[p] = picks[p]
    merged = picks_in[0].astype(f32)
    for q in range(1, 4):
        merged = merged + picks_in[q].astype(f32)
    band[p, pl.ds(pl.multiple_of(z * chunk, chunk), chunk), :] = merged.astype(bf16)

    def ring(block, halves, send, recv, arrived):
        def hop(s, left):
            at = lax.rem(z + (s - 1 if left else nz + 1 - s), nz)
            nxt = lax.rem(z + (nz - 1 if left else 1), nz)
            ref = halves(at, int(left)) if s == hops else block(at)
            i = (s - 1) * 2 + int(left)
            return remote(ref, ref, send.at[i], recv.at[i], d, nxt * 4 + p)

        hop(1, False).start()
        hop(1, True).start()
        arrived(0)
        for s in range(1, hops):
            hop(s, False).wait_recv()
            hop(s + 1, False).start()
            hop(s, True).wait_recv()
            hop(s + 1, True).start()
            arrived(s)
            arrived(nz - s)
        hop(hops, False).wait_recv()
        hop(hops, True).wait_recv()
        arrived(hops)

        def drain():
            for s in range(1, hops + 1):
                hop(s, False).wait_send()
                hop(s, True).wait_send()

        return drain

    def band_x(k, sender):
        zz = lax.rem(z + nz - k, nz)
        ref = band.at[p if sender else p_x, pl.ds(zz * chunk, chunk), :]
        return remote(ref, ref, bx_s.at[k], bx_r.at[k], d, z * 4 + p_x)

    drain_band = ring(
        lambda zz: band.at[p, pl.ds(zz * chunk, chunk), :],
        lambda zz, i: band.at[p, pl.ds(zz * chunk + i * (chunk // 2), chunk // 2), :],
        bz_s,
        bz_r,
        lambda k: band_x(k, True).start(),
    )

    def band_c(i, q):
        return remote(band.at[q], band.at[q], bc_s.at[i], bc_r.at[i], d, z * 4 + p_c)

    band_c(0, p).start()

    def reduce_copy(g):
        return remote(part.at[g], rs_in.at[d], rs_s.at[g], rs_r.at[d], g, r)

    def spread(side, q):
        for i in range(gq):
            y = dot(r_p[...], band[q, :, i * 256 : (i + 1) * 256]).astype(bf16)
            for t in range(2):
                row = (side * 2 * gq + 2 * i + t) * tok
                for e in range(CH):
                    xs[row : row + tok, e * 128 : (e + 1) * 128] = y[
                        e * tok : (e + 1) * tok, t * 128 : (t + 1) * 128
                    ]

    def project(pair_of_quarters):
        out = dot(xs[...], wbd[...]).astype(bf16)
        for side, q in enumerate(pair_of_quarters):
            for i in range(gq):
                g = q * gq + i
                for u in range(U):
                    row = (side * 2 * gq + 2 * i + u // 4) * tok
                    part[g, u * tok : (u + 1) * tok, :] = out[
                        row : row + tok, (u % 4) * CZ : (u % 4 + 1) * CZ
                    ]

                @pl.when(g != d)
                def _():
                    reduce_copy(g).start()

    spread(0, p)
    band_c(0, p_c).wait_recv()
    spread(1, p_c)
    for k in range(nz):
        band_x(k, False).wait_recv()
    band_c(1, p_x).start()
    project((p, p_c))
    spread(0, p_x)
    band_c(1, p_xc).wait_recv()
    spread(1, p_xc)
    project((p_x, p_xc))
    rs_in[d] = part[d]

    tb_own_c.wait_recv()
    tb_x_c.wait_recv()
    chain = chain_v[...]
    key_at = lax.broadcasted_iota(jnp.int32, (level, keys), 1)
    query_at = lax.broadcasted_iota(jnp.int32, (level, keys), 0) + z * level
    chain_f = chain.astype(f32)
    own = jnp.sum(jnp.where(key_at == query_at, chain_f, 0.0), axis=1, keepdims=True)
    differ = (own != chain_f).astype(f32)
    for h in range(H):
        for q in range(4):
            row = h * level + q * tok
            bias_f[row : row + tok, :] = (
                tb[q, h].astype(f32) + off_ref[h] * differ[q * tok : (q + 1) * tok, :]
            )

    for k in range(1, nd):
        src = lax.rem(d + k, nd)
        remote(part.at[src], rs_in.at[src], rs_s.at[src], rs_r.at[src], src, r).wait()

    total = rs_in[0].astype(f32)
    for k in range(1, nd):
        total = total + rs_in[k].astype(f32)
    pair = (total * (1.0 / (seqs * nd)) + ob[...]).astype(bf16)
    pair_ref[...] = pair.reshape(U, tok, CZ)
    value = pair.astype(f32)
    centred = value - jnp.mean(value, axis=1, keepdims=True)
    variance = jnp.mean(centred * centred, axis=1, keepdims=True)
    rows_out[...] = (centred * lax.rsqrt(variance + EPS)).astype(bf16).reshape(U, tok, CZ)

    mine = pl.ds(pl.multiple_of(r * tok, tok), tok)

    def rows_copy(q, src_p):
        at = pl.ds((z * 4 + src_p) * tok, tok)
        return remote(
            rows_out.at[pl.ds(q * 2, 2)], nb.at[:, at, :], ex_s.at[q], ex_r.at[src_p], d, z * 4 + q
        )

    for q in others:
        rows_copy(q, p).start()
    for i in range(2):
        nb[i, mine, :] = rows_out[2 * p + i]
    for q in others:
        rows_copy(q, q).wait_recv()

    drain_rows = ring(
        lambda zz: nb.at[:, pl.ds(zz * level, level), :],
        lambda zz, i: nb.at[i, pl.ds(zz * level, level), :],
        nz_s,
        nz_r,
        lambda k: None,
    )

    head_lane = lax.broadcasted_iota(jnp.int32, (level, CZ), 1) // DH
    for i in range(2):
        rows = nb[i]
        near = nb[i, pl.ds(pl.multiple_of(z * level, level), level), :]
        queries = dot(near, wqkvg[:, :CZ]).astype(bf16)
        gate = jax.nn.sigmoid(dot(near, wqkvg[:, 3 * CZ :]).astype(bf16).astype(f32))
        attended = jnp.zeros((level, CZ), f32)
        for h in range(H):
            own_head = jnp.where(head_lane == h, queries, jnp.zeros_like(queries))
            key_side = (dot_t(own_head, wqkvg[:, CZ : 2 * CZ]) * (DH**-0.5)).astype(bf16)
            scores = dot_t(key_side, rows) + bias_f[h * level : (h + 1) * level, :]
            top = jnp.max(scores, axis=1, keepdims=True)
            weights = jnp.exp(scores - top)
            denom = jnp.sum(weights, axis=1, keepdims=True)
            mixed = dot(weights.astype(bf16), rows) / denom
            values = dot(mixed.astype(bf16), wqkvg[:, 2 * CZ : 3 * CZ])
            attended = jnp.where(head_lane == h, values, attended)
        gated = (gate * attended).astype(bf16)
        ub[i] = dot(gated, wout[...]).astype(bf16)

    def upd_copy(q, src_p):
        return remote(
            ub.at[:, pl.ds(q * tok, tok), :],
            upd_in.at[src_p],
            up_s.at[q],
            up_r.at[src_p],
            d,
            z * 4 + q,
        )

    for q in others:
        upd_copy(q, p).start()
    upd_in[p] = ub[:, pl.ds(pl.multiple_of(p * tok, tok), tok), :]
    for q in others:
        upd_copy(q, q).wait_recv()
    for q in range(4):
        for i in range(2):
            upd_ref[2 * q + i] = upd_in[q, i]

    tb_own_x.wait_send()
    tb_own_c.wait_send()
    tb_x_c.wait_send()
    drain_band()
    for k in range(nz):
        band_x(k, True).wait_send()
    band_c(0, p).wait_send()
    band_c(1, p_x).wait_send()
    drain_rows()
    for q in others:
        rows_copy(q, p).wait_send()
        upd_copy(q, p).wait_send()


def body(
    nd,
    nr,
    alignment_left,
    alignment_right,
    window_starts,
    outer_product_weight,
    outer_product_bias,
    query_key_value_gate_weight,
    output_weight,
    triangle_pair_bias,
    residue_chain,
    interchain_offset,
):
    seqs, cols = alignment_left.shape
    tok = cols // CH
    nz = nr // 4
    chunk = seqs // nz
    quarter = nd // 4 * U * CH
    keys = nr * tok
    anywhere = pl.BlockSpec(memory_space=pl.ANY)
    vmem = pl.BlockSpec(memory_space=pltpu.VMEM)
    smem = pl.BlockSpec(memory_space=pltpu.SMEM)
    sem = pltpu.SemaphoreType.DMA
    out = jax.ShapeDtypeStruct((U, tok, CZ), bf16)
    return pl.pallas_call(
        functools.partial(kernel, nd, nr),
        out_shape=(out, out),
        in_specs=[smem, smem] + [anywhere] * 8,
        out_specs=(vmem, vmem),
        scratch_shapes=[
            pltpu.VMEM((seqs, cols), bf16),
            pltpu.VMEM((CH * CH, CZ), bf16),
            pltpu.VMEM((1, CZ), f32),
            pltpu.VMEM((CZ, 4 * CZ), bf16),
            pltpu.VMEM((CZ, CZ), bf16),
            pltpu.VMEM((1, keys), jnp.int32),
            pltpu.VMEM((4, H, tok, keys), bf16),
            pltpu.VMEM((nz, chunk, cols), bf16),
            pltpu.VMEM((nz * cols // 128, chunk, 128), bf16),
            pltpu.VMEM((4, chunk, quarter), bf16),
            pltpu.VMEM((4, chunk, quarter), bf16),
            pltpu.VMEM((4, seqs, quarter), bf16),
            pltpu.VMEM((seqs // 128, cols, 128), f32),
            pltpu.VMEM((cols, seqs), bf16),
            pltpu.VMEM((CH * CH, CZ), f32),
            pltpu.VMEM((CH * 128, 4 * CZ), bf16),
            pltpu.VMEM((H * 4 * tok, keys), f32),
            pltpu.VMEM((nd // 2 * 2 * tok, CH * 128), bf16),
            pltpu.VMEM((nd, U * tok, CZ), bf16),
            pltpu.VMEM((nd, U * tok, CZ), bf16),
            pltpu.VMEM((U, tok, CZ), bf16),
            pltpu.VMEM((2, keys, CZ), bf16),
            pltpu.VMEM((2, 4 * tok, CZ), bf16),
            pltpu.VMEM((4, 2, tok, CZ), bf16),
            sem((8,)),
            sem((nz,)),
            sem((nz,)),
            sem((3,)),
            sem((3,)),
            sem((4,)),
            sem((4,)),
            sem((nz,)),
            sem((nz,)),
            sem((nz,)),
            sem((nz,)),
            sem((2,)),
            sem((2,)),
            sem((nd,)),
            sem((nd,)),
            sem((4,)),
            sem((4,)),
            sem((nz,)),
            sem((nz,)),
            sem((4,)),
            sem((4,)),
        ],
        compiler_params=pltpu.CompilerParams(
            collective_id=0, has_side_effects=True, vmem_limit_bytes=VMEM_BYTES
        ),
        cost_estimate=pl.CostEstimate(
            flops=4_000_000_000, bytes_accessed=4_000_000, transcendentals=1_100_000
        ),
    )(
        window_starts,
        interchain_offset,
        alignment_left,
        alignment_right,
        outer_product_weight,
        outer_product_bias.reshape(1, CZ),
        query_key_value_gate_weight,
        output_weight,
        triangle_pair_bias,
        residue_chain.reshape(1, keys),
    )


def solution(mesh):
    in_specs = (
        P("depth", "res"),
        P("depth", "res"),
        P(),
        P(),
        P(),
        P(),
        P(),
        P(None, "res", None),
        P(),
        P(),
    )
    out_specs = (P("depth", "res", None), P("depth", "res", None))
    return jax.shard_map(
        functools.partial(body, mesh.shape["depth"], mesh.shape["res"]),
        mesh=mesh,
        in_specs=in_specs,
        out_specs=out_specs,
        check_vma=False,
    )
```

time: 91.8 us -> 82.8 us (0.902); the launches traced: 91.3 us -> 81.2 us
  local copies, waits for them, and re-layouts: 8.25 us -> 2.14 us
  Pallas kernels: 82.3 us -> 78.4 us
    unnamed x22 -> x4, local copies, waits for them, and re-layouts: 8.25 us -> 2.14 us
    pallas_call x1, Pallas kernels: 82.3 us -> 78.4 us  [body(): pl.pallas_call(functools.partial(kernel, nd, nr), out_shape=(out, out), i...]
where the time goes in v2:
time: 82.8 us; the launch traced here: 81.2 us
  Pallas kernels  78.4 us (95%)
  local copies, waits for them, and re-layouts  2.14 us (3%)
    pallas_call x1, Pallas kernels, body(): pl.pallas_call(functools.partial(kernel, nd, nr), out_shape=(out, out), i...  78.4 us
    unnamed x4, local copies, waits for them, and re-layouts  2.14 us

profile of v2, /device:TPU:1, one launch (start us, length us, event | category | flops | bytes accessed | tf_op | source)
XLA Modules:
  0.0 81.2 jit_solution(14401256280485222023)
XLA Ops:
  0.6 78.4 %shard_map.113 = (bf16[8,32,128]{2,1,0:T(8,128)(2,1)}, bf16[8,32,128]{2,1,0:T(8,128)(2,1)}) custom-call(s32[8]{0:T(128)} %ws_ref.1, f32[4]{0:T(128)} %off_ref.1, bf16[256,1024]{1,0:T(8,128)(2,1)} %left_hbm.1, bf16[256,1024]{1,0:T(8,128)(2,1)} %right_hbm.1, bf16[1024,128]{1,0:T(8,128)(2,1)} %w_hbm.1, f32[1,128]{1,0:T(1,128)} %bitcast.3, ...), custom_call_target="tpu_custom_call" | custom-call | flops 4000000000 | bytes 4000000 | tf_op jit(solution)/shard_map/pallas_call | solution.py:448
  79.1 0.0 copy-start
  79.1 1.5 %copy.14 = bf16[8,32,128]{2,1,0:T(8,128)(2,1)} copy(bf16[8,32,128]{2,1,0:T(8,128)(2,1)} %get-tuple-element.4) | data formatting | bytes 131072
  80.6 0.0 copy-done
  80.6 0.6 copy.15
Async XLA Ops:
  79.1 1.5 %copy-start = (bf16[8,32,128]{2,1,0:T(8,128)(2,1)S(1)}, bf16[8,32,128]{2,1,0:T(8,128)(2,1)}, u32[]{:S(2)}) copy-start(bf16[8,32,128]{2,1,0:T(8,128)(2,1)} %get-tuple-element.5) | copy-start | bytes 196612

commit v3 on v2

--- a/solution.py
+++ b/solution.py
@@ -64,6 +64,7 @@
     rs_in,
     rows_out,
     nb,
+    qp,
     ub,
     upd_in,
     in_sem,
@@ -91,7 +92,6 @@
     seqs, cols = left_hbm.shape
     tok = cols // CH
     nz = nr // 4
-    hops = nz // 2
     chunk = seqs // nz
     groups = nd
     quarter = groups // 4 * U * CH
@@ -227,47 +227,38 @@
         merged = merged + picks_in[q].astype(f32)
     band[p, pl.ds(pl.multiple_of(z * chunk, chunk), chunk), :] = merged.astype(bf16)
 
-    def ring(block, halves, send, recv, arrived):
-        def hop(s, left):
-            at = lax.rem(z + (s - 1 if left else nz + 1 - s), nz)
-            nxt = lax.rem(z + (nz - 1 if left else 1), nz)
-            ref = halves(at, int(left)) if s == hops else block(at)
-            i = (s - 1) * 2 + int(left)
-            return remote(ref, ref, send.at[i], recv.at[i], d, nxt * 4 + p)
-
-        hop(1, False).start()
-        hop(1, True).start()
-        arrived(0)
-        for s in range(1, hops):
-            hop(s, False).wait_recv()
-            hop(s + 1, False).start()
-            hop(s, True).wait_recv()
-            hop(s + 1, True).start()
-            arrived(s)
-            arrived(nz - s)
-        hop(hops, False).wait_recv()
-        hop(hops, True).wait_recv()
-        arrived(hops)
+    near = sorted(range(1, nz), key=lambda k: min(k, nz - k))
+
+    def gather(block, send, recv):
+        def copy(k, back):
+            zz = lax.rem(z + (nz - k if back else k), nz)
+            ref = block(zz if back else z)
+            return remote(ref, ref, send.at[k], recv.at[k], d, zz * 4 + p)
+
+        for k in near:
+            copy(k, False).start()
+
+        def arrive(k):
+            copy(k, True).wait_recv()
 
         def drain():
-            for s in range(1, hops + 1):
-                hop(s, False).wait_send()
-                hop(s, True).wait_send()
-
-        return drain
+            for k in near:
+                copy(k, False).wait_send()
+
+        return arrive, drain
 
     def band_x(k, sender):
         zz = lax.rem(z + nz - k, nz)
         ref = band.at[p if sender else p_x, pl.ds(zz * chunk, chunk), :]
         return remote(ref, ref, bx_s.at[k], bx_r.at[k], d, z * 4 + p_x)
 
-    drain_band = ring(
-        lambda zz: band.at[p, pl.ds(zz * chunk, chunk), :],
-        lambda zz, i: band.at[p, pl.ds(zz * chunk + i * (chunk // 2), chunk // 2), :],
-        bz_s,
-        bz_r,
-        lambda k: band_x(k, True).start(),
+    band_arrive, drain_band = gather(
+        lambda zz: band.at[p, pl.ds(zz * chunk, chunk), :], bz_s, bz_r
     )
+    band_x(0, True).start()
+    for k in near:
+        band_arrive(k)
+        band_x(k, True).start()
 
     def band_c(i, q):
         return remote(band.at[q], band.at[q], bc_s.at[i], bc_r.at[i], d, z * 4 + p_c)
@@ -359,33 +350,50 @@
     for q in others:
         rows_copy(q, q).wait_recv()
 
-    drain_rows = ring(
-        lambda zz: nb.at[:, pl.ds(zz * level, level), :],
-        lambda zz, i: nb.at[i, pl.ds(zz * level, level), :],
-        nz_s,
-        nz_r,
-        lambda k: None,
+    rows_arrive, drain_rows = gather(
+        lambda zz: nb.at[:, pl.ds(zz * level, level), :], nz_s, nz_r
     )
 
     head_lane = lax.broadcasted_iota(jnp.int32, (level, CZ), 1) // DH
+    gates = []
     for i in range(2):
-        rows = nb[i]
-        near = nb[i, pl.ds(pl.multiple_of(z * level, level), level), :]
-        queries = dot(near, wqkvg[:, :CZ]).astype(bf16)
-        gate = jax.nn.sigmoid(dot(near, wqkvg[:, 3 * CZ :]).astype(bf16).astype(f32))
+        here = nb[i, pl.ds(pl.multiple_of(z * level, level), level), :]
+        queries = dot(here, wqkvg[:, :CZ]).astype(bf16)
+        gates.append(jax.nn.sigmoid(dot(here, wqkvg[:, 3 * CZ :]).astype(bf16).astype(f32)))
+        for h in range(H):
+            own_head = jnp.where(head_lane == h, queries, jnp.zeros_like(queries))
+            key_side = dot_t(own_head, wqkvg[:, CZ : 2 * CZ]) * (DH**-0.5)
+            qp[i, h * level : (h + 1) * level, :] = key_side.astype(bf16)
+
+    top, denom, mixed = [None, None], [None, None], [None, None]
+    for ks in [(0,)] + [(k, nz - k) for k in range(1, nz // 2)] + [(nz // 2,)]:
+        for k in ks:
+            if k:
+                rows_arrive(k)
+        ats = [pl.ds(pl.multiple_of(lax.rem(z + nz - k, nz) * level, level), level) for k in ks]
+        offsets = jnp.concatenate([bias_f[:, at] for at in ats], axis=1)
+        for i in range(2):
+            rows = jnp.concatenate([nb[i, at, :] for at in ats], axis=0)
+            scores = dot_t(qp[i], rows) + offsets
+            peak = jnp.max(scores, axis=1, keepdims=True)
+            if ks == (0,):
+                weights = jnp.exp(scores - peak)
+                denom[i] = jnp.sum(weights, axis=1, keepdims=True)
+                mixed[i] = dot(weights.astype(bf16), rows)
+            else:
+                peak = jnp.maximum(peak, top[i])
+                shrink = jnp.exp(top[i] - peak)
+                weights = jnp.exp(scores - peak)
+                denom[i] = denom[i] * shrink + jnp.sum(weights, axis=1, keepdims=True)
+                mixed[i] = mixed[i] * shrink + dot(weights.astype(bf16), rows)
+            top[i] = peak
+
+    for i in range(2):
+        values = dot((mixed[i] / denom[i]).astype(bf16), wqkvg[:, 2 * CZ : 3 * CZ])
         attended = jnp.zeros((level, CZ), f32)
         for h in range(H):
-            own_head = jnp.where(head_lane == h, queries, jnp.zeros_like(queries))
-            key_side = (dot_t(own_head, wqkvg[:, CZ : 2 * CZ]) * (DH**-0.5)).astype(bf16)
-            scores = dot_t(key_side, rows) + bias_f[h * level : (h + 1) * level, :]
-            top = jnp.max(scores, axis=1, keepdims=True)
-            weights = jnp.exp(scores - top)
-            denom = jnp.sum(weights, axis=1, keepdims=True)
-            mixed = dot(weights.astype(bf16), rows) / denom
-            values = dot(mixed.astype(bf16), wqkvg[:, 2 * CZ : 3 * CZ])
-            attended = jnp.where(head_lane == h, values, attended)
-        gated = (gate * attended).astype(bf16)
-        ub[i] = dot(gated, wout[...]).astype(bf16)
+            attended = jnp.where(head_lane == h, values[h * level : (h + 1) * level, :], attended)
+        ub[i] = dot((gates[i] * attended).astype(bf16), wout[...]).astype(bf16)
 
     def upd_copy(q, src_p):
         return remote(
@@ -473,6 +481,7 @@
             pltpu.VMEM((nd, U * tok, CZ), bf16),
             pltpu.VMEM((U, tok, CZ), bf16),
             pltpu.VMEM((2, keys, CZ), bf16),
+            pltpu.VMEM((2, H * 4 * tok, CZ), bf16),
             pltpu.VMEM((2, 4 * tok, CZ), bf16),
             pltpu.VMEM((4, 2, tok, CZ), bf16),
             sem((8,)),

time: 82.8 us -> 77.2 us (0.932)
  Pallas kernels: 78.4 us -> 73.5 us
    pallas_call x1, Pallas kernels: 78.4 us -> 73.5 us  [body(): pl.pallas_call(functools.partial(kernel, nd, nr), out_shape=(out, out), i...]
where the time goes in v3:
time: 77.2 us; the launch traced here: 76.3 us
  Pallas kernels  73.5 us (95%)
  local copies, waits for them, and re-layouts  2.14 us (3%)
    pallas_call x1, Pallas kernels, body(): pl.pallas_call(functools.partial(kernel, nd, nr), out_shape=(out, out), i...  73.5 us
    unnamed x4, local copies, waits for them, and re-layouts  2.14 us

profile of v3, /device:TPU:1, one launch (start us, length us, event | category | flops | bytes accessed | tf_op | source)
XLA Modules:
  0.0 76.3 jit_solution(6190682438359776827)
XLA Ops:
  0.6 73.5 %shard_map.113 = (bf16[8,32,128]{2,1,0:T(8,128)(2,1)}, bf16[8,32,128]{2,1,0:T(8,128)(2,1)}) custom-call(s32[8]{0:T(128)} %ws_ref.1, f32[4]{0:T(128)} %off_ref.1, bf16[256,1024]{1,0:T(8,128)(2,1)} %left_hbm.1, bf16[256,1024]{1,0:T(8,128)(2,1)} %right_hbm.1, bf16[1024,128]{1,0:T(8,128)(2,1)} %w_hbm.1, f32[1,128]{1,0:T(1,128)} %bitcast.3, ...), custom_call_target="tpu_custom_call" | custom-call | flops 4000000000 | bytes 4000000 | tf_op jit(solution)/shard_map/pallas_call | solution.py:456
  74.2 0.0 copy-start
  74.2 1.5 %copy.14 = bf16[8,32,128]{2,1,0:T(8,128)(2,1)} copy(bf16[8,32,128]{2,1,0:T(8,128)(2,1)} %get-tuple-element.4) | data formatting | bytes 131072
  75.7 0.0 copy-done
  75.7 0.6 copy.15
Async XLA Ops:
  74.2 1.5 %copy-start = (bf16[8,32,128]{2,1,0:T(8,128)(2,1)S(1)}, bf16[8,32,128]{2,1,0:T(8,128)(2,1)}, u32[]{:S(2)}) copy-start(bf16[8,32,128]{2,1,0:T(8,128)(2,1)} %get-tuple-element.5) | copy-start | bytes 196612

commit v4 on v3

--- a/solution.py
+++ b/solution.py
@@ -62,7 +62,8 @@
     xs,
     part,
     rs_in,
-    rows_out,
+    pair_out,
+    pair_in,
     nb,
     qp,
     ub,
@@ -76,14 +77,14 @@
     pk_r,
     bz_s,
     bz_r,
-    bx_s,
-    bx_r,
+    rx_s,
+    rx_r,
     bc_s,
     bc_r,
     rs_s,
     rs_r,
-    ex_s,
-    ex_r,
+    pr_s,
+    pr_r,
     nz_s,
     nz_r,
     up_s,
@@ -94,8 +95,8 @@
     nz = nr // 4
     chunk = seqs // nz
     groups = nd
-    quarter = groups // 4 * U * CH
     gq = groups // 4
+    gh = groups // 2
     tiles_dev = cols // 128
     keys = nr * tok
     level = 4 * tok
@@ -129,13 +130,19 @@
     for q in others:
         pl.semaphore_signal(barrier, inc=1, device_id=(d, z * 4 + q), device_id_type=MESH)
     for k in range(1, nd):
-        pl.semaphore_signal(barrier, inc=1, device_id=(lax.rem(d + k, nd), r), device_id_type=MESH)
+        for e in range(2):
+            pl.semaphore_signal(
+                barrier,
+                inc=1,
+                device_id=(lax.rem(d + k, nd), z * 4 + d // gh * 2 + e),
+                device_id_type=MESH,
+            )
 
     inputs = [
         pltpu.make_async_copy(src, dst, in_sem.at[i])
         for i, (src, dst) in enumerate(
             (
-                (right_hbm, right),
+                (right_hbm, right.at[x]),
                 (w_hbm, w),
                 (ob_hbm, ob),
                 (wqkvg_hbm, wqkvg),
@@ -148,7 +155,8 @@
     ]
     for copy in inputs:
         copy.start()
-    pl.semaphore_wait(barrier, nz - 1 + 3 + nd - 1)
+    apart = (d // gh - x) * (d // gh - x)
+    pl.semaphore_wait(barrier, nz - 1 + 3 + 4 * (gh - 1) + 4 * apart)
 
     def scatter_copy(k):
         zz = lax.rem(z + k, nz)
@@ -165,23 +173,27 @@
     for k in order:
         scatter_copy(k).start()
 
+    right_copy = remote(right_hbm, right.at[x], rx_s.at[0], rx_r.at[0], d, z * 4 + p_x)
+    right_copy.start()
+
     for copy in inputs:
         copy.wait()
     tb_own_x = remote(tb.at[p], tb.at[p], tb_s.at[0], tb_r.at[0], d, z * 4 + p_x)
     tb_own_c = remote(tb.at[p], tb.at[p], tb_s.at[1], tb_r.at[1], d, z * 4 + p_c)
     tb_x_c = remote(tb.at[p_x], tb.at[p_x], tb_s.at[2], tb_r.at[2], d, z * 4 + p_c)
-    tb_own_x.start()
-    tb_own_c.start()
-
-    for q in range(seqs // 128):
-        r_t[q] = jnp.transpose(right[q * 128 : (q + 1) * 128, :].astype(f32))
+
+    def turn_right(b):
+        for q in range(seqs // 128):
+            r_t[q] = jnp.transpose(right[b, q * 128 : (q + 1) * 128, :].astype(f32))
+        for i in range(CH):
+            row = pl.ds(pl.multiple_of((2 * i + b) * tok, tok), tok)
+            for q in range(seqs // 128):
+                r_p[row, q * 128 : (q + 1) * 128] = r_t[q, pl.ds(i, tok, stride=CH), :].astype(bf16)
+
+    turn_right(x)
     w_f[...] = w[...].astype(f32)
     wbd[...] = jnp.zeros_like(wbd)
     for i in range(CH):
-        for q in range(seqs // 128):
-            r_p[i * tok : (i + 1) * tok, q * 128 : (q + 1) * 128] = r_t[
-                q, pl.ds(i, tok, stride=CH), :
-            ].astype(bf16)
         w_i = w_f[pl.ds(i, CH, stride=CH), :].astype(bf16)
         for b in range(4):
             wbd[i * 128 + b * CH : i * 128 + (b + 1) * CH, b * CZ : (b + 1) * CZ] = w_i
@@ -216,8 +228,10 @@
     ]
     for copy in picks_out:
         copy.start()
-    tb_own_x.wait_recv()
-    tb_x_c.start()
+    right_copy.wait()
+    tb_own_x.start()
+    tb_own_c.start()
+    turn_right(1 - x)
     for q, copy in zip(others, picks_out):
         copy.wait_send()
         remote(picks.at[q], picks_in.at[q], pk_s.at[q], pk_r.at[q], d, z * 4 + q).wait_recv()
@@ -225,7 +239,7 @@
     merged = picks_in[0].astype(f32)
     for q in range(1, 4):
         merged = merged + picks_in[q].astype(f32)
-    band[p, pl.ds(pl.multiple_of(z * chunk, chunk), chunk), :] = merged.astype(bf16)
+    band[c, pl.ds(pl.multiple_of(z * chunk, chunk), chunk), :] = merged.astype(bf16)
 
     near = sorted(range(1, nz), key=lambda k: min(k, nz - k))
 
@@ -247,64 +261,57 @@
 
         return arrive, drain
 
-    def band_x(k, sender):
-        zz = lax.rem(z + nz - k, nz)
-        ref = band.at[p if sender else p_x, pl.ds(zz * chunk, chunk), :]
-        return remote(ref, ref, bx_s.at[k], bx_r.at[k], d, z * 4 + p_x)
-
     band_arrive, drain_band = gather(
-        lambda zz: band.at[p, pl.ds(zz * chunk, chunk), :], bz_s, bz_r
+        lambda zz: band.at[c, pl.ds(zz * chunk, chunk), :], bz_s, bz_r
     )
-    band_x(0, True).start()
     for k in near:
         band_arrive(k)
-        band_x(k, True).start()
-
-    def band_c(i, q):
-        return remote(band.at[q], band.at[q], bc_s.at[i], bc_r.at[i], d, z * 4 + p_c)
-
-    band_c(0, p).start()
-
-    def reduce_copy(g):
-        return remote(part.at[g], rs_in.at[d], rs_s.at[g], rs_r.at[d], g, r)
-
-    def spread(side, q):
+
+    def band_c(q):
+        return remote(band.at[q], band.at[q], bc_s.at[0], bc_r.at[0], d, z * 4 + p_c)
+
+    band_c(c).start()
+
+    def reduce_copy(i, q, g, depth, e):
+        return remote(
+            part.at[i, q], rs_in.at[depth * 2 + e], rs_s.at[i * 4 + q], rs_r.at[depth * 2 + e], g, z * 4 + q
+        )
+
+    def outer(e):
         for i in range(gq):
-            y = dot(r_p[...], band[q, :, i * 256 : (i + 1) * 256]).astype(bf16)
+            y = dot(r_p[...], band[e, :, i * 256 : (i + 1) * 256]).astype(bf16)
             for t in range(2):
-                row = (side * 2 * gq + 2 * i + t) * tok
-                for e in range(CH):
-                    xs[row : row + tok, e * 128 : (e + 1) * 128] = y[
-                        e * tok : (e + 1) * tok, t * 128 : (t + 1) * 128
+                row = (2 * i + t) * 2 * tok
+                for b in range(CH):
+                    xs[row : row + 2 * tok, b * 128 : (b + 1) * 128] = y[
+                        b * 2 * tok : (b + 1) * 2 * tok, t * 128 : (t + 1) * 128
                     ]
-
-    def project(pair_of_quarters):
         out = dot(xs[...], wbd[...]).astype(bf16)
-        for side, q in enumerate(pair_of_quarters):
-            for i in range(gq):
-                g = q * gq + i
-                for u in range(U):
-                    row = (side * 2 * gq + 2 * i + u // 4) * tok
-                    part[g, u * tok : (u + 1) * tok, :] = out[
-                        row : row + tok, (u % 4) * CZ : (u % 4 + 1) * CZ
-                    ]
-
-                @pl.when(g != d)
+        for i in range(gq):
+            at = e * gq + i
+            g = x * gh + at
+            for q in range(4):
+                for n in range(2):
+                    u = 2 * q + n
+                    for b in range(2):
+                        row = ((2 * i + u // 4) * 2 + b) * tok
+                        part[at, q, n, b] = out[row : row + tok, (u % 4) * CZ : (u % 4 + 1) * CZ]
+
+                here = jnp.logical_and(g == d, q == p)
+
+                @pl.when(jnp.logical_not(here))
                 def _():
-                    reduce_copy(g).start()
-
-    spread(0, p)
-    band_c(0, p_c).wait_recv()
-    spread(1, p_c)
-    for k in range(nz):
-        band_x(k, False).wait_recv()
-    band_c(1, p_x).start()
-    project((p, p_c))
-    spread(0, p_x)
-    band_c(1, p_xc).wait_recv()
-    spread(1, p_xc)
-    project((p_x, p_xc))
-    rs_in[d] = part[d]
+                    reduce_copy(at, q, g, d, c).start()
+
+                @pl.when(here)
+                def _():
+                    rs_in[d * 2 + c] = part[at, q]
+
+    outer(c)
+    band_c(1 - c).wait_recv()
+    tb_own_x.wait_recv()
+    tb_x_c.start()
+    outer(1 - c)
 
     tb_own_c.wait_recv()
     tb_x_c.wait_recv()
@@ -321,38 +328,74 @@
                 tb[q, h].astype(f32) + off_ref[h] * differ[q * tok : (q + 1) * tok, :]
             )
 
-    for k in range(1, nd):
-        src = lax.rem(d + k, nd)
-        remote(part.at[src], rs_in.at[src], rs_s.at[src], rs_r.at[src], src, r).wait()
-
-    total = rs_in[0].astype(f32)
-    for k in range(1, nd):
-        total = total + rs_in[k].astype(f32)
-    pair = (total * (1.0 / (seqs * nd)) + ob[...]).astype(bf16)
-    pair_ref[...] = pair.reshape(U, tok, CZ)
-    value = pair.astype(f32)
-    centred = value - jnp.mean(value, axis=1, keepdims=True)
-    variance = jnp.mean(centred * centred, axis=1, keepdims=True)
-    rows_out[...] = (centred * lax.rsqrt(variance + EPS)).astype(bf16).reshape(U, tok, CZ)
-
-    mine = pl.ds(pl.multiple_of(r * tok, tok), tok)
-
-    def rows_copy(q, src_p):
-        at = pl.ds((z * 4 + src_p) * tok, tok)
+    def reduced(depth, e):
         return remote(
-            rows_out.at[pl.ds(q * 2, 2)], nb.at[:, at, :], ex_s.at[q], ex_r.at[src_p], d, z * 4 + q
+            part.at[0, 0],
+            rs_in.at[depth * 2 + e],
+            rs_s.at[0],
+            rs_r.at[depth * 2 + e],
+            depth,
+            z * 4 + d // gh * 2 + e,
+        )
+
+    for e in range(2):
+        for k in range(nd):
+            source = lax.rem(d + k, nd)
+            if k == 0:
+
+                @pl.when(jnp.logical_not(jnp.logical_and(d // gh == x, c == e)))
+                def _():
+                    reduced(d, e).wait_recv()
+
+            else:
+                reduced(source, e).wait_recv()
+
+        total = rs_in[e].astype(f32)
+        for k in range(1, nd):
+            total = total + rs_in[2 * k + e].astype(f32)
+        total = total.reshape(4 * tok, CZ)
+        pair = (total * (1.0 / (seqs * nd)) + ob[...]).astype(bf16)
+        value = pair.astype(f32)
+        centred = value - jnp.mean(value, axis=1, keepdims=True)
+        variance = jnp.mean(centred * centred, axis=1, keepdims=True)
+        normed = (centred * lax.rsqrt(variance + EPS)).astype(bf16)
+        for n in range(2):
+            for b in range(2):
+                piece = slice((2 * n + b) * tok, (2 * n + b + 1) * tok)
+                to = pl.ds(pl.multiple_of((z * 4 + 2 * b + e) * tok, tok), tok)
+                nb[n, to, :] = normed[piece]
+                pair_out[2 * b + e, n] = pair[piece]
+
+    def rows_copy(k, to, at, i=None):
+        rows = pl.ds(lax.rem(z + nz + at, nz) * level, level)
+        ref = nb.at[:, rows, :] if i is None else nb.at[i, rows, :]
+        return remote(ref, ref, nz_s.at[k], nz_r.at[k], d, lax.rem(z + nz + to, nz) * 4 + p)
+
+    if nz == 8:
+        first = [rows_copy(k, k, 0) for k in (2, 6, 1, 7)]
+        onward = {
+            2: [rows_copy(3, 1, -2), rows_copy(4, 2, -2, 0)],
+            6: [rows_copy(5, -1, 2), rows_copy(0, -2, 2, 1)],
+        }
+        landing = {k: [rows_copy(k, 0, -k)] for k in (1, 2, 3, 5, 6, 7)}
+        landing[4] = [rows_copy(4, 0, 4, 0), rows_copy(0, 0, 4, 1)]
+        turns = [(0,), (2, 6), (1, 7), (3, 5), (4,)]
+    else:
+        first = [rows_copy(k, k, 0) for k in near]
+        onward = {}
+        landing = {k: [rows_copy(k, 0, -k)] for k in near}
+        turns = [(0,)] + [(k, nz - k) for k in range(1, nz // 2)] + [(nz // 2,)]
+    for copy in first:
+        copy.start()
+
+    def pair_copy(q, src_p):
+        return remote(
+            pair_out.at[q], pair_in.at[src_p], pr_s.at[q], pr_r.at[src_p], d, z * 4 + q
         )
 
     for q in others:
-        rows_copy(q, p).start()
-    for i in range(2):
-        nb[i, mine, :] = rows_out[2 * p + i]
-    for q in others:
-        rows_copy(q, q).wait_recv()
-
-    rows_arrive, drain_rows = gather(
-        lambda zz: nb.at[:, pl.ds(zz * level, level), :], nz_s, nz_r
-    )
+        pair_copy(q, p).start()
+    pair_in[p] = pair_out[p]
 
     head_lane = lax.broadcasted_iota(jnp.int32, (level, CZ), 1) // DH
     gates = []
@@ -366,10 +409,12 @@
             qp[i, h * level : (h + 1) * level, :] = key_side.astype(bf16)
 
     top, denom, mixed = [None, None], [None, None], [None, None]
-    for ks in [(0,)] + [(k, nz - k) for k in range(1, nz // 2)] + [(nz // 2,)]:
+    for ks in turns:
         for k in ks:
-            if k:
-                rows_arrive(k)
+            for copy in landing.get(k, ()):
+                copy.wait_recv()
+            for copy in onward.get(k, ()):
+                copy.start()
         ats = [pl.ds(pl.multiple_of(lax.rem(z + nz - k, nz) * level, level), level) for k in ks]
         offsets = jnp.concatenate([bias_f[:, at] for at in ats], axis=1)
         for i in range(2):
@@ -409,6 +454,11 @@
         upd_copy(q, p).start()
     upd_in[p] = ub[:, pl.ds(pl.multiple_of(p * tok, tok), tok), :]
     for q in others:
+        pair_copy(q, q).wait_recv()
+    for q in range(4):
+        for i in range(2):
+            pair_ref[2 * q + i] = pair_in[q, i]
+    for q in others:
         upd_copy(q, q).wait_recv()
     for q in range(4):
         for i in range(2):
@@ -418,13 +468,18 @@
     tb_own_c.wait_send()
     tb_x_c.wait_send()
     drain_band()
-    for k in range(nz):
-        band_x(k, True).wait_send()
-    band_c(0, p).wait_send()
-    band_c(1, p_x).wait_send()
-    drain_rows()
+    band_c(c).wait_send()
+    for i in range(gh):
+        for q in range(4):
+
+            @pl.when(jnp.logical_not(jnp.logical_and(x * gh + i == d, q == p)))
+            def _():
+                reduce_copy(i, q, x * gh + i, d, c).wait_send()
+
+    for copy in first + [copy for copies in onward.values() for copy in copies]:
+        copy.wait_send()
     for q in others:
-        rows_copy(q, p).wait_send()
+        pair_copy(q, p).wait_send()
         upd_copy(q, p).wait_send()
 
 
@@ -459,7 +514,7 @@
         in_specs=[smem, smem] + [anywhere] * 8,
         out_specs=(vmem, vmem),
         scratch_shapes=[
-            pltpu.VMEM((seqs, cols), bf16),
+            pltpu.VMEM((2, seqs, cols), bf16),
             pltpu.VMEM((CH * CH, CZ), bf16),
             pltpu.VMEM((1, CZ), f32),
             pltpu.VMEM((CZ, 4 * CZ), bf16),
@@ -470,16 +525,17 @@
             pltpu.VMEM((nz * cols // 128, chunk, 128), bf16),
             pltpu.VMEM((4, chunk, quarter), bf16),
             pltpu.VMEM((4, chunk, quarter), bf16),
-            pltpu.VMEM((4, seqs, quarter), bf16),
+            pltpu.VMEM((2, seqs, quarter), bf16),
             pltpu.VMEM((seqs // 128, cols, 128), f32),
-            pltpu.VMEM((cols, seqs), bf16),
+            pltpu.VMEM((2 * cols, seqs), bf16),
             pltpu.VMEM((CH * CH, CZ), f32),
             pltpu.VMEM((CH * 128, 4 * CZ), bf16),
             pltpu.VMEM((H * 4 * tok, keys), f32),
-            pltpu.VMEM((nd // 2 * 2 * tok, CH * 128), bf16),
-            pltpu.VMEM((nd, U * tok, CZ), bf16),
-            pltpu.VMEM((nd, U * tok, CZ), bf16),
-            pltpu.VMEM((U, tok, CZ), bf16),
+            pltpu.VMEM((nd // 4 * 2 * 2 * tok, CH * 128), bf16),
+            pltpu.VMEM((nd // 2, 4, 2, 2, tok, CZ), bf16),
+            pltpu.VMEM((2 * nd, 2, 2, tok, CZ), bf16),
+            pltpu.VMEM((4, 2, tok, CZ), bf16),
+            pltpu.VMEM((4, 2, tok, CZ), bf16),
             pltpu.VMEM((2, keys, CZ), bf16),
             pltpu.VMEM((2, H * 4 * tok, CZ), bf16),
             pltpu.VMEM((2, 4 * tok, CZ), bf16),
@@ -493,12 +549,12 @@
             sem((4,)),
             sem((nz,)),
             sem((nz,)),
-            sem((nz,)),
-            sem((nz,)),
-            sem((2,)),
-            sem((2,)),
-            sem((nd,)),
-            sem((nd,)),
+            sem((1,)),
+            sem((1,)),
+            sem((1,)),
+            sem((1,)),
+            sem((2 * nd,)),
+            sem((2 * nd,)),
             sem((4,)),
             sem((4,)),
             sem((nz,)),

time: 77.2 us -> 67.5 us (0.87)
  Pallas kernels: 73.5 us -> 64.3 us
    pallas_call x1, Pallas kernels: 73.5 us -> 64.3 us  [body(): pl.pallas_call(functools.partial(kernel, nd, nr), out_shape=(out, out), i...]
where the time goes in v4:
time: 67.5 us; the launch traced here: 67.1 us
  Pallas kernels  64.3 us (95%)
  local copies, waits for them, and re-layouts  2.14 us (3%)
    pallas_call x1, Pallas kernels, body(): pl.pallas_call(functools.partial(kernel, nd, nr), out_shape=(out, out), i...  64.3 us
    unnamed x4, local copies, waits for them, and re-layouts  2.14 us

profile of v4, /device:TPU:1, one launch (start us, length us, event | category | flops | bytes accessed | tf_op | source)
XLA Modules:
  0.0 67.1 jit_solution(4945774103609885282)
XLA Ops:
  0.6 64.3 %shard_map.113 = (bf16[8,32,128]{2,1,0:T(8,128)(2,1)}, bf16[8,32,128]{2,1,0:T(8,128)(2,1)}) custom-call(s32[8]{0:T(128)} %ws_ref.1, f32[4]{0:T(128)} %off_ref.1, bf16[256,1024]{1,0:T(8,128)(2,1)} %left_hbm.1, bf16[256,1024]{1,0:T(8,128)(2,1)} %right_hbm.1, bf16[1024,128]{1,0:T(8,128)(2,1)} %w_hbm.1, f32[1,128]{1,0:T(1,128)} %bitcast.3, ...), custom_call_target="tpu_custom_call" | custom-call | flops 4000000000 | bytes 4000000 | tf_op jit(solution)/shard_map/pallas_call | solution.py:511
  64.9 0.0 copy-start
  65.0 1.5 %copy.14 = bf16[8,32,128]{2,1,0:T(8,128)(2,1)} copy(bf16[8,32,128]{2,1,0:T(8,128)(2,1)} %get-tuple-element.4) | data formatting | bytes 131072
  66.5 0.0 copy-done
  66.5 0.6 copy.15
Async XLA Ops:
  64.9 1.5 %copy-start = (bf16[8,32,128]{2,1,0:T(8,128)(2,1)S(1)}, bf16[8,32,128]{2,1,0:T(8,128)(2,1)}, u32[]{:S(2)}) copy-start(bf16[8,32,128]{2,1,0:T(8,128)(2,1)} %get-tuple-element.5) | copy-start | bytes 196612

commit v5 on v4

--- a/solution.py
+++ b/solution.py
@@ -228,10 +228,6 @@
     ]
     for copy in picks_out:
         copy.start()
-    right_copy.wait()
-    tb_own_x.start()
-    tb_own_c.start()
-    turn_right(1 - x)
     for q, copy in zip(others, picks_out):
         copy.wait_send()
         remote(picks.at[q], picks_in.at[q], pk_s.at[q], pk_r.at[q], d, z * 4 + q).wait_recv()
@@ -264,6 +260,24 @@
     band_arrive, drain_band = gather(
         lambda zz: band.at[c, pl.ds(zz * chunk, chunk), :], bz_s, bz_r
     )
+
+    def bias_of(q):
+        chain_f = chain_v[...].astype(f32)
+        key_at = lax.broadcasted_iota(jnp.int32, (tok, keys), 1)
+        query_at = lax.broadcasted_iota(jnp.int32, (tok, keys), 0) + (z * level + q * tok)
+        own = jnp.sum(jnp.where(key_at == query_at, chain_f, 0.0), axis=1, keepdims=True)
+        differ = (own != chain_f).astype(f32)
+        for h in range(H):
+            at = pl.ds(pl.multiple_of(h * level + q * tok, tok), tok)
+            bias_f[at, :] = tb[q, h].astype(f32) + off_ref[h] * differ
+
+    tb_own_c.start()
+    right_copy.wait()
+    tb_own_x.start()
+    turn_right(1 - x)
+    bias_of(p)
+    tb_own_c.wait_recv()
+    bias_of(p_c)
     for k in near:
         band_arrive(k)
 
@@ -309,24 +323,12 @@
 
     outer(c)
     band_c(1 - c).wait_recv()
+    outer(1 - c)
     tb_own_x.wait_recv()
     tb_x_c.start()
-    outer(1 - c)
-
-    tb_own_c.wait_recv()
+    bias_of(p_x)
     tb_x_c.wait_recv()
-    chain = chain_v[...]
-    key_at = lax.broadcasted_iota(jnp.int32, (level, keys), 1)
-    query_at = lax.broadcasted_iota(jnp.int32, (level, keys), 0) + z * level
-    chain_f = chain.astype(f32)
-    own = jnp.sum(jnp.where(key_at == query_at, chain_f, 0.0), axis=1, keepdims=True)
-    differ = (own != chain_f).astype(f32)
-    for h in range(H):
-        for q in range(4):
-            row = h * level + q * tok
-            bias_f[row : row + tok, :] = (
-                tb[q, h].astype(f32) + off_ref[h] * differ[q * tok : (q + 1) * tok, :]
-            )
+    bias_of(p_xc)
 
     def reduced(depth, e):
         return remote(
@@ -366,24 +368,23 @@
                 nb[n, to, :] = normed[piece]
                 pair_out[2 * b + e, n] = pair[piece]
 
-    def rows_copy(k, to, at, i=None):
-        rows = pl.ds(lax.rem(z + nz + at, nz) * level, level)
-        ref = nb.at[:, rows, :] if i is None else nb.at[i, rows, :]
-        return remote(ref, ref, nz_s.at[k], nz_r.at[k], d, lax.rem(z + nz + to, nz) * 4 + p)
+    def rows_copy(k, to, at, i):
+        ref = nb.at[i, pl.ds(lax.rem(z + nz + at, nz) * level, level), :]
+        n = k * 2 + i
+        return remote(ref, ref, nz_s.at[n], nz_r.at[n], d, lax.rem(z + nz + to, nz) * 4 + p)
 
     if nz == 8:
-        first = [rows_copy(k, k, 0) for k in (2, 6, 1, 7)]
+        first = [rows_copy(k, k, 0, i) for ks in ((2, 6), (1, 7)) for i in range(2) for k in ks]
         onward = {
-            2: [rows_copy(3, 1, -2), rows_copy(4, 2, -2, 0)],
-            6: [rows_copy(5, -1, 2), rows_copy(0, -2, 2, 1)],
+            (2, 0): [rows_copy(3, 1, -2, 0), rows_copy(4, 2, -2, 0)],
+            (2, 1): [rows_copy(3, 1, -2, 1)],
+            (6, 0): [rows_copy(5, -1, 2, 0)],
+            (6, 1): [rows_copy(5, -1, 2, 1), rows_copy(4, -2, 2, 1)],
         }
-        landing = {k: [rows_copy(k, 0, -k)] for k in (1, 2, 3, 5, 6, 7)}
-        landing[4] = [rows_copy(4, 0, 4, 0), rows_copy(0, 0, 4, 1)]
         turns = [(0,), (2, 6), (1, 7), (3, 5), (4,)]
     else:
-        first = [rows_copy(k, k, 0) for k in near]
+        first = [rows_copy(k, k, 0, i) for k in near for i in range(2)]
         onward = {}
-        landing = {k: [rows_copy(k, 0, -k)] for k in near}
         turns = [(0,)] + [(k, nz - k) for k in range(1, nz // 2)] + [(nz // 2,)]
     for copy in first:
         copy.start()
@@ -410,11 +411,12 @@
 
     top, denom, mixed = [None, None], [None, None], [None, None]
     for ks in turns:
-        for k in ks:
-            for copy in landing.get(k, ()):
-                copy.wait_recv()
-            for copy in onward.get(k, ()):
-                copy.start()
+        if ks != (0,):
+            for i in range(2):
+                for k in ks:
+                    rows_copy(k, 0, -k, i).wait_recv()
+                    for copy in onward.get((k, i), ()):
+                        copy.start()
         ats = [pl.ds(pl.multiple_of(lax.rem(z + nz - k, nz) * level, level), level) for k in ks]
         offsets = jnp.concatenate([bias_f[:, at] for at in ats], axis=1)
         for i in range(2):
@@ -557,8 +559,8 @@
             sem((2 * nd,)),
             sem((4,)),
             sem((4,)),
-            sem((nz,)),
-            sem((nz,)),
+            sem((2 * nz,)),
+            sem((2 * nz,)),
             sem((4,)),
             sem((4,)),
         ],

time: 67.5 us -> 66.9 us (level)
  no operation moved by 1% of the time
where the time goes in v5:
time: 66.9 us; the launch traced here: 66.8 us
  Pallas kernels  64 us (96%)
  local copies, waits for them, and re-layouts  2.14 us (3%)
    pallas_call x1, Pallas kernels, body(): pl.pallas_call(functools.partial(kernel, nd, nr), out_shape=(out, out), i...  64 us
    unnamed x4, local copies, waits for them, and re-layouts  2.14 us

profile of v5, /device:TPU:1, one launch (start us, length us, event | category | flops | bytes accessed | tf_op | source)
XLA Modules:
  0.0 66.8 jit_solution(2727581043501827341)
XLA Ops:
  0.6 64.0 %shard_map.113 = (bf16[8,32,128]{2,1,0:T(8,128)(2,1)}, bf16[8,32,128]{2,1,0:T(8,128)(2,1)}) custom-call(s32[8]{0:T(128)} %ws_ref.1, f32[4]{0:T(128)} %off_ref.1, bf16[256,1024]{1,0:T(8,128)(2,1)} %left_hbm.1, bf16[256,1024]{1,0:T(8,128)(2,1)} %right_hbm.1, bf16[1024,128]{1,0:T(8,128)(2,1)} %w_hbm.1, f32[1,128]{1,0:T(1,128)} %bitcast.3, ...), custom_call_target="tpu_custom_call" | custom-call | flops 4000000000 | bytes 4000000 | tf_op jit(solution)/shard_map/pallas_call | solution.py:513
  64.6 0.0 copy-start
  64.6 1.5 %copy.14 = bf16[8,32,128]{2,1,0:T(8,128)(2,1)} copy(bf16[8,32,128]{2,1,0:T(8,128)(2,1)} %get-tuple-element.4) | data formatting | bytes 131072
  66.1 0.0 copy-done
  66.1 0.6 copy.15
Async XLA Ops:
  64.6 1.5 %copy-start = (bf16[8,32,128]{2,1,0:T(8,128)(2,1)S(1)}, bf16[8,32,128]{2,1,0:T(8,128)(2,1)}, u32[]{:S(2)}) copy-start(bf16[8,32,128]{2,1,0:T(8,128)(2,1)} %get-tuple-element.5) | copy-start | bytes 196612
